TPU v7x, 32 devices: a whole 2x2x4 slice. The times are simulated.
32 devices in a mesh: dp: 4 (over y, x), ctx: 8 (over z, core).
Axes of the slice: x: 2, y: 2, z: 4, core: 2. Of those that a mesh axis runs over, the one named last changes fastest.
Arguments:
- tokens: bfloat16 [4, 4096, 2048], P('dp', 'ctx'), may hold values from -6 to 6
- w_query: bfloat16 [2048, 128], replicated, may hold values from -0.125 to 0.125
- w_key: bfloat16 [2048, 128], replicated, may hold values from -0.125 to 0.125
- w_value: bfloat16 [2048, 512], replicated, may hold values from -0.125 to 0.125
- w_out: bfloat16 [512, 2048], replicated, may hold values from -0.25 to 0.25
- grad_out: bfloat16 [4, 4096, 2048], P('dp', 'ctx'), may hold values from -6 to 6
Outputs:
- grad_tokens: bfloat16 [4, 4096, 2048], P('dp', 'ctx')
- grad_qkv: float32 [2048, 768], P(('dp', 'ctx'))
- grad_w_out: float32 [512, 2048], P(('dp', 'ctx'))
All inputs are finite; a program needn't handle non-finite values.
Results may differ from a plain program's by a relative error of at most 0.013.
Values sent between devices are 32-bit elements; how exact they have to be, the bound alone decides.
A program may use at most 256 MiB of HBM per device.

v0:
```python
import math

import jax
import jax.numpy as jnp
from jax import lax
from jax.sharding import PartitionSpec as P

HEADS = 8
FEAT = 16
HDIM = 64


SQRT_HALF = 0.7071067811865476
HIGH = lax.Precision.HIGHEST


def carried_in(value, axis, join, neutral, backward):
    count, mine = (lax.axis_size(axis), lax.axis_index(axis))
    pieces = jax.tree.map(lambda part: lax.all_gather(part, axis), value)
    if backward:
        pieces = jax.tree.map(lambda part: part[::-1], pieces)
        mine = count - 1 - mine
    subtotal = jax.tree.map(
        lambda part, zero: jnp.full_like(part, 0) + jnp.asarray(zero, part.dtype), value, neutral
    )

    def turn(position, subtotal):
        longer = join(subtotal, jax.tree.map(lambda part: part[position], pieces))
        return jax.tree.map(lambda new, old: jnp.where(position < mine, new, old), longer, subtotal)

    return lax.fori_loop(0, count - 1, turn, subtotal)


def feature_map(vectors):
    ones = jnp.ones(vectors.shape[:-1] + (1,), vectors.dtype)
    width = vectors.shape[-1]
    square = (vectors[..., :, None] * vectors[..., None, :]).reshape(
        vectors.shape[:-1] + (width * width,)
    )
    return jnp.concatenate([ones, vectors, square * SQRT_HALF], axis=-1)


def block_state(key_vec, value_vec):
    lifted = feature_map(key_vec)
    state = jnp.einsum("the,thd->hed", lifted, value_vec, precision=HIGH)
    normal = jnp.sum(lifted, axis=0)
    return (state, normal)


def block_output(query_vec, key_vec, value_vec, prior_state, prior_norm):
    count = query_vec.shape[0]
    scores = jnp.einsum("thf,shf->hts", query_vec, key_vec, precision=HIGH)
    causal = (
        lax.broadcasted_iota(jnp.int32, (count, count), 0)
        >= lax.broadcasted_iota(jnp.int32, (count, count), 1)
    ).astype(scores.dtype)
    kernel = (1.0 + scores + 0.5 * scores * scores) * causal
    lifted = feature_map(query_vec)
    numerator = jnp.einsum("hts,shd->thd", kernel, value_vec, precision=HIGH) + jnp.einsum(
        "the,hed->thd", lifted, prior_state, precision=HIGH
    )
    denominator = jnp.sum(kernel, axis=2).T + jnp.einsum(
        "the,he->th", lifted, prior_norm, precision=HIGH
    )
    return numerator / denominator[..., None]


def add_pair(earlier, later):
    return (earlier[0] + later[0], earlier[1] + later[1])


def transposed_dot(left, weight):
    return lax.dot_general(
        left, weight, (((1,), (1,)), ((), ())), preferred_element_type=jnp.float32
    )


def row_term(left, right, factor):
    return (
        lax.dot_general(left, right, (((0,), (0,)), ((), ())), preferred_element_type=jnp.float32)
        * factor
    )


def shards(tokens, w_query, w_key, w_value, w_out, grad_out):
    token_rows = tokens.reshape(-1, tokens.shape[-1])
    grad_rows = grad_out.reshape(-1, grad_out.shape[-1])
    count = token_rows.shape[0]
    queries = (jnp.dot(token_rows, w_query, preferred_element_type=jnp.float32) * 0.5).astype(
        jnp.bfloat16
    )
    keys_own = (jnp.dot(token_rows, w_key, preferred_element_type=jnp.float32) * 0.5).astype(
        jnp.bfloat16
    )
    values_own = jnp.dot(token_rows, w_value, preferred_element_type=jnp.float32).astype(
        jnp.bfloat16
    )
    query_vec = queries.astype(jnp.float32).reshape(count, HEADS, FEAT)
    key_vec = keys_own.astype(jnp.float32).reshape(count, HEADS, FEAT)
    value_vec = values_own.astype(jnp.float32).reshape(count, HEADS, HDIM)
    key_state, key_norm = block_state(key_vec, value_vec)
    empty_pair = (jnp.zeros_like(key_state), jnp.zeros_like(key_norm))
    prior_state, prior_norm = carried_in((key_state, key_norm), "ctx", add_pair, empty_pair, False)
    grad_attn = transposed_dot(grad_rows, w_out)
    outputs, backward = jax.vjp(
        block_output, query_vec, key_vec, value_vec, prior_state, prior_norm
    )
    attended = outputs.reshape(count, -1).astype(jnp.bfloat16)
    grad_query, grad_key_own, grad_value_own, grad_state, grad_norm = backward(
        grad_attn.reshape(count, HEADS, HDIM)
    )
    later_state, later_norm = carried_in((grad_state, grad_norm), "ctx", add_pair, empty_pair, True)
    unused, state_back = jax.vjp(block_state, key_vec, value_vec)
    grad_key_far, grad_value_far = state_back((later_state, later_norm))
    proj_query = (grad_query * 0.5).reshape(count, -1).astype(jnp.bfloat16)
    proj_key = ((grad_key_own + grad_key_far) * 0.5).reshape(count, -1).astype(jnp.bfloat16)
    proj_value = (grad_value_own + grad_value_far).reshape(count, -1).astype(jnp.bfloat16)
    grad_tokens = (
        transposed_dot(proj_query, w_query)
        + transposed_dot(proj_key, w_key)
        + transposed_dot(proj_value, w_value)
    ).astype(jnp.bfloat16)
    groups_dp = lax.axis_size("dp")
    groups_ctx = lax.axis_size("ctx")
    factor = 1.0 / math.sqrt(groups_dp * groups_ctx * count)
    stacked = jnp.concatenate([proj_query, proj_key, proj_value], axis=1)
    grad_qkv = lax.psum_scatter(
        row_term(token_rows, stacked, factor), ("dp", "ctx"), scatter_dimension=0, tiled=True
    )
    grad_w_out = lax.psum_scatter(
        row_term(attended, grad_rows, factor), ("dp", "ctx"), scatter_dimension=0, tiled=True
    )
    return (grad_tokens.reshape(tokens.shape), grad_qkv, grad_w_out)


def solution(mesh):
    placed = (P("dp", "ctx", None), P(), P(), P(), P(), P("dp", "ctx", None))
    return jax.shard_map(
        shards,
        mesh=mesh,
        in_specs=placed,
        out_specs=(P("dp", "ctx", None), P(("dp", "ctx"), None), P(("dp", "ctx"), None)),
        check_vma=False,
    )
```

profile of v0, /device:TPU:0, one launch (start us, length us, event | category | flops | bytes accessed | tf_op | source)
XLA Modules:
  0.0 476.9 jit_solution(9518753086861074425)
XLA Ops:
  7.2 1.5 copy-done
  8.8 2.0 bitcast_convert_fusion
  11.5 1.3 fusion.27
  13.6 3.8 fusion.6
  17.5 3.0 fusion.5
  20.6 17.2 %all-gather.1 = f32[64,273]{1,0:T(8,128)} all-gather(f32[8,273]{1,0:T(8,128)S(1)} %fusion.5), channel_id=3, replica_groups=mesh['dp'=4,'ctx'=8] {'ctx'}, dimensions={0}, use_global_device_ids=true | all-gather | bytes 78624 | tf_op jit(solution)/shard_map/all_gather | solution.py:19
  38.8 2.6 multiply_multiply_fusion.1
  41.4 2.3 fusion.21
  43.7 5.1 %fusion.11 = (f32[8,512]{1,0:T(8,128)}, f32[8,512,512]{1,2,0:T(8,128)}) fusion(f32[512,512]{0,1:T(8,128)S(1)} %fusion.48, bf16[512,8,16]{0,2,1:T(8,128)(2,1)S(1)} %bitcast.160, bf16[512,8,16]{0,2,1:T(8,128)(2,1)S(1)} %bitcast.162), kind=kOutput, calls=%fused_computation.31 | convolution fusion | flops 79687680 | bytes 9715712 | tf_op jit(solution)/shard_map/jvp(thf,shf->hts)/dot_general | solution.py:52
  48.8 36.6 %all-gather.7.cloned.1.call-done = f32[64,273,64]{1,2,0:T(8,128)} async-done(((f32[8,273,64]{1,2,0:T(8,128)}), f32[64,273,64]{1,2,0:T(8,128)}) %all-gather.7.cloned.1.call-update) | async-done | bytes 4472848 | tf_op jit(solution)/shard_map/all_gather | solution.py:19
  85.4 45.9 %while.32 = (s32[]{:T(128)}, f32[8,273,64]{2,1,0:T(8,128)}, f32[8,273]{1,0:T(8,128)S(1)}, s32[]{:T(128)}, f32[8,8,273,64]{2,3,1,0:T(8,128)}, /*index=5*/f32[8,8,273]{2,1,0:T(8,128)}, s32[]{:T(128)}, s32[]{:T(128)}) while((s32[]{:T(128)}, f32[8,273,64]{2,1,0:T(8,128)}, f32[8,273]{1,0:T(8,128)S(1)}, s32[]{:T(128)}, ...), condition=%wide.region_3.4_spmd.clone, body=%wide.region_2.3_spmd.clone.sunk | while | flops 425884 | bytes 3940051 | solution.py:31
  85.4 2.1 constant_dynamic-slice_fusion.2
  87.5 1.5 copy.58
  90.8 2.1 constant_dynamic-slice_fusion.2
  92.9 1.5 copy.58
  94.5 2.4 add_select_fusion.8
  97.6 2.1 constant_dynamic-slice_fusion.2
  99.7 1.5 copy.58
  101.2 2.4 add_select_fusion.8
  104.3 2.1 constant_dynamic-slice_fusion.2
  106.4 1.5 copy.58
  108.0 2.4 add_select_fusion.8
  111.1 2.1 constant_dynamic-slice_fusion.2
  113.2 1.5 copy.58
  114.7 2.4 add_select_fusion.8
  117.8 2.1 constant_dynamic-slice_fusion.2
  119.9 1.5 copy.58
  121.4 2.4 add_select_fusion.8
  124.5 2.1 constant_dynamic-slice_fusion.2
  126.6 1.5 copy.58
  128.2 2.4 add_select_fusion.8
  131.3 5.3 %fusion.58 = f32[8,1,512]{2,1,0:T(1,128)S(1)} fusion(f32[8,273,1]{1,0,2:T(8,128)S(1)} %bitcast.159, f32[512,8,256]{0,2,1:T(8,128)} %bitcast.145, f32[512,8,16]{0,2,1:T(8,128)} %copy-done.7, f32[273]{0:T(512)S(1)} %pad.6.clone), kind=kOutput, calls=%fused_computation.82 | convolution fusion | flops 15654912 | bytes 4482660 | tf_op jit(solution)/shard_map/jvp(the,he->th)/dot_general | solution.py:62
  137.2 7.2 %fusion.67 = f32[8,273,64]{1,2,0:T(8,128)} fusion(f32[512,8,64]{0,2,1:T(8,128)} %fusion.21, f32[8,512]{1,0:T(8,128)S(1)} %get-tuple-element.316, f32[512,8,256]{0,2,1:T(8,128)S(1)} %bitcast.147, f32[512,8,16]{0,2,1:T(8,128)S(1)} %copy-done.8, f32[273]{0:T(512)S(1)} %pad.6.clone), kind=kOutput, calls=%fused_computation.93 | convolution fusion | flops 861282304 | bytes 6081604 | tf_op jit(solution)/shard_map/transpose(jvp(the,hed->thd))/dot_general | solution.py:59
  144.5 8.3 %fusion.9 = f32[8,64,512]{2,1,0:T(8,128)S(1)} fusion(bf16[512,8,64]{0,2,1:T(8,128)(2,1)} %bitcast.165, f32[8,512,512]{1,2,0:T(8,128)} %get-tuple-element.322, f32[512,512]{0,1:T(8,128)} %copy-done.23), kind=kOutput, calls=%fused_computation.30 | convolution fusion | flops 1621098496 | bytes 11010048 | tf_op jit(solution)/shard_map/jvp(hts,shd->thd)/dot_general | solution.py:59
  152.9 4.0 divide_convert_fusion
  157.5 3.3 convolution_multiply_fusion
  160.8 5.7 %add_bitcast_fusion.1 = f32[512,8,273]{0,2,1:T(8,128)S(1)} fusion(f32[8,273]{1,0:T(8,128)S(1)} %get-tuple-element.223, f32[8,512]{1,0:T(8,128)S(1)} %get-tuple-element.319, f32[8,273,64]{2,1,0:T(8,128)} %get-tuple-element.224, f32[512,8,64]{0,2,1:T(8,128)} %fusion.21, f32[8,512]{1,0:T(8,128)} %copy-done.33), kind=kOutput, calls=%fused_computation.14 | convolution fusion | flops 861282304 | bytes 6122016 | tf_op jit(solution)/shard_map/transpose(jvp(the,hed->thd))/dot_general | solution.py:59
  167.3 1.6 copy-done.2
  169.0 3.4 multiply_reduce_fusion.3
  172.6 6.3 %fusion.56 = f32[8,1,273]{2,1,0:T(1,128)S(1)} fusion(f32[8,512,1]{1,0,2:T(8,128)} %get-tuple-element.320, f32[512,8,256]{0,2,1:T(8,128)} %bitcast.146, f32[512,8,16]{0,2,1:T(8,128)} %copy-done.7, f32[273]{0:T(512)S(1)} %pad.6.clone), kind=kOutput, calls=%fused_computation.76 | convolution fusion | flops 15654912 | bytes 4482660 | tf_op jit(solution)/shard_map/transpose(jvp(the,he->th))/dot_general | solution.py:62
  178.9 15.6 %all-gather.3 = f32[64,273]{1,0:T(8,128)} all-gather(f32[8,273]{1,0:T(8,128)S(1)} %bitcast.172), channel_id=5, replica_groups=mesh['dp'=4,'ctx'=8] {'ctx'}, dimensions={0}, use_global_device_ids=true | all-gather | bytes 78624 | tf_op jit(solution)/shard_map/all_gather | solution.py:19
  194.5 1.5 rev.7
  196.0 9.6 %fusion.2 = f32[8,512,512]{1,2,0:T(8,128)S(1)} fusion(f32[8,512,512]{1,2,0:T(8,128)} %get-tuple-element.322, f32[8,512]{1,0:T(8,128)S(1)} %get-tuple-element.319, f32[512,512]{0,1:T(8,128)} %copy-done.23, bf16[512,8,64]{0,2,1:T(8,128)(2,1)} %bitcast.166, f32[512,8,64]{0,2,1:T(8,128)} %fusion.21, f32[8,512]{1,0:T(8,128)} %copy-done.33), kind=kOutput, calls=%fused_computation.9 | convolution fusion | flops 1627652096 | bytes 19431424 | tf_op jit(solution)/shard_map/transpose(jvp(hts,shd->thd))/dot_general | solution.py:59
  205.7 5.0 %fusion.40 = bf16[512,8,16]{0,2,1:T(8,128)(2,1)} fusion(f32[8,512,512]{1,2,0:T(8,128)S(1)} %fusion.2, bf16[512,8,16]{0,2,1:T(8,128)(2,1)S(1)} %bitcast.163, f32[512,8,16]{0,2,1:T(8,128)S(1)} %copy-done.22, f32[512,8,16]{0,2,1:T(8,128)S(1)} %copy-done.21, f32[512,8,273]{0,2,1:T(8,128)} %copy-done.2), kind=kOutput, calls=%fused_computation.57 | convolution fusion | flops 402980864 | bytes 9437184 | tf_op jit(solution)/shard_map/transpose(jvp(thf,shf->hts))/dot_general | solution.py:52
  210.8 12.2 %fusion.7 = f32[8,64,512]{2,1,0:T(8,128)} fusion(f32[8,512,512]{1,2,0:T(8,128)} %get-tuple-element.322, f32[512,512]{0,1:T(8,128)S(1)} %copy-done.24, f32[512,8,64]{0,2,1:T(8,128)S(1)} %copy-done.26, f32[8,512]{1,0:T(8,128)S(1)} %copy-done.34), kind=kOutput, calls=%fused_computation.29 | convolution fusion | flops 1621360640 | bytes 11550720 | tf_op jit(solution)/shard_map/transpose(jvp(hts,shd->thd))/dot_general | solution.py:59
  222.9 8.9 %copy.28 = f32[8,8,273,64]{3,2,1,0:T(8,128)} copy(f32[8,8,273,64]{2,3,1,0:T(8,128)} %bitcast.151) | data formatting | bytes 8945664 | tf_op jit(solution)/shard_map/all_gather | solution.py:19
  231.8 7.9 %rev.6 = f32[8,8,273,64]{3,2,1,0:T(8,128)} reverse(f32[8,8,273,64]{3,2,1,0:T(8,128)} %copy.28), dimensions={0} | reverse | bytes 8945664 | tf_op jit(solution)/shard_map/rev | solution.py:21
  239.7 16.1 %while.33 = (s32[]{:T(128)}, f32[8,273,64]{2,1,0:T(8,128)S(1)}, f32[8,273]{1,0:T(8,128)S(1)}, s32[]{:T(128)}, f32[8,8,273,64]{3,2,1,0:T(8,128)}, /*index=5*/f32[8,8,273]{2,1,0:T(8,128)}, s32[]{:T(128)}, s32[]{:T(128)}) while((s32[]{:T(128)}, f32[8,273,64]{2,1,0:T(8,128)S(1)}, f32[8,273]{1,0:T(8,128)S(1)}, s32[]{:T(128)}, ...), condition=%wide.region_8.9_spmd.clone, body=%wide.region_7.8_spmd.clone.sunk | while | flops 425884 | bytes 1703635 | solution.py:31
  239.7 1.6 add_select_fusion.10
  242.0 1.6 add_select_fusion.10
  244.3 1.5 add_select_fusion.10
  246.5 1.5 add_select_fusion.10
  248.8 1.6 add_select_fusion.10
  251.1 1.6 add_select_fusion.10
  253.4 1.5 add_select_fusion.10
  255.8 6.5 %fusion.26 = bf16[8,64,512]{2,1,0:T(8,128)(2,1)S(1)} fusion(f32[8,64,512]{2,1,0:T(8,128)} %fusion.7, f32[8,273,64]{2,1,0:T(8,128)S(1)} %get-tuple-element.226, f32[512,8,256]{0,2,1:T(8,128)} %bitcast.142, f32[512,8,16]{0,2,1:T(8,128)S(1)} %get-tuple-element.323, f32[273]{0:T(512)S(1)} %pad.6.clone), kind=kOutput, calls=%fused_computation.47 | convolution fusion | flops 861544448 | bytes 6589508 | tf_op jit(solution)/shard_map/transpose(jvp(the,thd->hed))/dot_general | solution.py:45
  262.4 2.0 add_bitcast_fusion
  265.2 2.7 multiply_reduce_fusion.1
  268.1 4.2 fusion.41
  272.3 4.5 multiply_bitcast_fusion
  276.7 6.6 %copy.46 = f32[2048,768]{1,0:T(8,128)} copy(f32[2048,768]{0,1:T(8,128)} %multiply_bitcast_fusion) | data formatting | bytes 12582912
  286.1 2.6 fusion.3
  288.8 64.0 %reduce-scatter.5.cloned.1.call-done = f32[16,2048]{1,0:T(8,128)} async-done(((f32[512,2048]{1,0:T(8,128)}), f32[16,2048]{1,0:T(8,128)}) %reduce-scatter.5.cloned.1.call-update) | async-done | bytes 131088 | tf_op jit(solution)/shard_map/reduce_scatter | solution.py:130
  352.8 117.1 %reduce-scatter.7.cloned.1.call-done = f32[64,768]{1,0:T(8,128)} async-done(((f32[2048,768]{1,0:T(8,128)}), f32[64,768]{1,0:T(8,128)}) %reduce-scatter.7.cloned.1.call-update) | async-done | bytes 196624
  (118 shorter events, 19.9 us)
Async XLA Ops:
  7.2 1.6 copy-start
  7.2 78.2 %all-gather.7.cloned.1.call-start = ((), (), s32[]{:S(2)}) async-start(), calls=%async_computation.3 | async-start | bytes 7077888 | tf_op jit(solution)/shard_map/all_gather | solution.py:19
  8.8 2.7 copy-start.13
  10.8 32.9 %copy-start.29 = (bf16[512,128]{0,1:T(8,128)(2,1)}, bf16[512,128]{0,1:T(8,128)(2,1)S(1)}, u32[]{:S(2)}) copy-start(bf16[512,128]{0,1:T(8,128)(2,1)S(1)} %get-tuple-element.324) | copy-start | bytes 393220
  11.5 2.0 copy-start.3
  12.8 0.8 copy-start.31
  17.4 20.5 %copy-start.17 = (bf16[2048,128]{1,0:T(8,128)(2,1)S(1)}, bf16[2048,128]{1,0:T(8,128)(2,1)}, u32[]{:S(2)}) copy-start(bf16[2048,128]{1,0:T(8,128)(2,1)} %param.11) | copy-start | bytes 1572868
  17.5 205.4 %all-gather.9.cloned.1.call-start = ((), (), s32[]{:S(2)}) async-start(), calls=%async_computation.4 | async-start | bytes 7077888 | tf_op jit(solution)/shard_map/all_gather | solution.py:19
  37.8 3.6 copy-start.15
  37.8 3.6 copy-start.37
  37.9 5.7 %copy-start.23 = (f32[512,512]{0,1:T(8,128)}, f32[512,512]{0,1:T(8,128)S(1)}, u32[]{:S(2)}) copy-start(f32[512,512]{0,1:T(8,128)S(1)} %fusion.48) | copy-start | bytes 3145732
  38.8 4.9 %copy-start.7 = (f32[512,8,16]{0,2,1:T(8,128)}, f32[512,8,16]{0,2,1:T(8,128)S(1)}, u32[]{:S(2)}) copy-start(f32[512,8,16]{0,2,1:T(8,128)S(1)} %get-tuple-element.325) | copy-start | bytes 786436
  38.8 4.9 %copy-start.27 = (bf16[512,128]{0,1:T(8,128)(2,1)}, bf16[512,128]{0,1:T(8,128)(2,1)S(1)}, u32[]{:S(2)}) copy-start(bf16[512,128]{0,1:T(8,128)(2,1)S(1)} %get-tuple-element.326) | copy-start | bytes 393220
  131.3 5.3 %copy-start.35 = (f32[8,512]{1,0:T(8,128)S(1)}, f32[8,512]{1,0:T(8,128)}, u32[]{:S(2)}) copy-start(f32[8,512]{1,0:T(8,128)} %get-tuple-element.321) | copy-start | bytes 49156
  131.3 5.9 %copy-start.5 = (f32[512,8,16,16]{0,3,2,1:T(8,128)S(1)}, f32[512,8,16,16]{0,3,2,1:T(8,128)}, u32[]{:S(2)}) copy-start(f32[512,8,16,16]{0,3,2,1:T(8,128)} %multiply_multiply_fusion.1) | copy-start | bytes 12582916
  131.3 5.9 %copy-start.8 = (f32[512,8,16]{0,2,1:T(8,128)S(1)}, f32[512,8,16]{0,2,1:T(8,128)}, u32[]{:S(2)}) copy-start(f32[512,8,16]{0,2,1:T(8,128)} %copy-done.7) | copy-start | bytes 786436
  137.1 15.7 %copy-start.33 = (f32[8,512]{1,0:T(8,128)}, f32[8,512]{1,0:T(8,128)S(1)}, u32[]{:S(2)}) copy-start(f32[8,512]{1,0:T(8,128)S(1)} %get-tuple-element.316) | copy-start | bytes 49156
  144.3 208.5 %reduce-scatter.5.cloned.1.call-start = ((), (), s32[]{:S(2)}) async-start(), calls=%async_computation.2 | async-start | bytes 4325376 | tf_op jit(solution)/shard_map/reduce_scatter | solution.py:130
  144.4 8.4 %copy-start.1 = (f32[8,273,64]{2,1,0:T(8,128)S(1)}, f32[8,273,64]{2,1,0:T(8,128)}, u32[]{:S(2)}) copy-start(f32[8,273,64]{2,1,0:T(8,128)} %get-tuple-element.224) | copy-start | bytes 1677316
  144.4 8.4 %copy-start.6 = (f32[512,8,16,16]{0,3,2,1:T(8,128)S(1)}, f32[512,8,16,16]{0,3,2,1:T(8,128)}, u32[]{:S(2)}) copy-start(f32[512,8,16,16]{0,3,2,1:T(8,128)} %multiply_multiply_fusion.1) | copy-start | bytes 12582916
  144.4 8.4 %copy-start.9 = (f32[512,8,16]{0,2,1:T(8,128)S(1)}, f32[512,8,16]{0,2,1:T(8,128)}, u32[]{:S(2)}) copy-start(f32[512,8,16]{0,2,1:T(8,128)} %copy-done.7) | copy-start | bytes 786436
  144.4 8.4 %copy-start.25 = (f32[512,8,64]{0,2,1:T(8,128)S(1)}, f32[512,8,64]{0,2,1:T(8,128)}, u32[]{:S(2)}) copy-start(f32[512,8,64]{0,2,1:T(8,128)} %fusion.21) | copy-start | bytes 3145732
  144.5 8.4 %copy-start.36 = (f32[512,8]{0,1:T(8,128)S(1)}, f32[512,8]{0,1:T(8,128)}, u32[]{:S(2)}) copy-start(f32[512,8]{0,1:T(8,128)} %get-tuple-element.315) | copy-start | bytes 49156
  152.9 4.6 copy-start.16
  166.5 2.4 copy-start.2
  166.5 2.4 copy-start.10
  172.4 297.5 %reduce-scatter.7.cloned.1.call-start = ((), (), s32[]{:S(2)}) async-start(), calls=%async_computation.5 | async-start | bytes 6488064
  196.0 9.6 %copy-start.21 = (f32[512,8,16]{0,2,1:T(8,128)S(1)}, f32[512,8,16]{0,2,1:T(8,128)}, u32[]{:S(2)}) copy-start(f32[512,8,16]{0,2,1:T(8,128)} %get-tuple-element.289) | copy-start | bytes 786436
  196.0 9.7 %copy-start.22 = (f32[512,8,16]{0,2,1:T(8,128)S(1)}, f32[512,8,16]{0,2,1:T(8,128)}, u32[]{:S(2)}) copy-start(f32[512,8,16]{0,2,1:T(8,128)} %get-tuple-element.290) | copy-start | bytes 786436
  196.0 9.7 %copy-start.30 = (bf16[512,128]{0,1:T(8,128)(2,1)S(1)}, bf16[512,128]{0,1:T(8,128)(2,1)}, u32[]{:S(2)}) copy-start(bf16[512,128]{0,1:T(8,128)(2,1)} %copy-done.29) | copy-start | bytes 393220
  205.7 5.1 %copy-start.4 = (f32[8,512,512]{1,2,0:T(8,128)}, f32[8,512,512]{1,2,0:T(8,128)S(1)}, u32[]{:S(2)}) copy-start(f32[8,512,512]{1,2,0:T(8,128)S(1)} %fusion.2) | copy-start | bytes 25165828
  205.7 5.1 %copy-start.24 = (f32[512,512]{0,1:T(8,128)S(1)}, f32[512,512]{0,1:T(8,128)}, u32[]{:S(2)}) copy-start(f32[512,512]{0,1:T(8,128)} %copy-done.23) | copy-start | bytes 3145732
  205.7 5.0 %copy-start.26 = (f32[512,8,64]{0,2,1:T(8,128)S(1)}, f32[512,8,64]{0,2,1:T(8,128)}, u32[]{:S(2)}) copy-start(f32[512,8,64]{0,2,1:T(8,128)} %fusion.21) | copy-start | bytes 3145732
  205.7 5.0 %copy-start.34 = (f32[8,512]{1,0:T(8,128)S(1)}, f32[8,512]{1,0:T(8,128)}, u32[]{:S(2)}) copy-start(f32[8,512]{1,0:T(8,128)} %copy-done.33) | copy-start | bytes 49156
  255.8 6.6 %copy-start.32 = (bf16[512,512]{0,1:T(8,128)(2,1)S(1)}, bf16[512,512]{0,1:T(8,128)(2,1)}, u32[]{:S(2)}) copy-start(bf16[512,512]{0,1:T(8,128)(2,1)} %copy-done.31) | copy-start | bytes 1572868
  262.3 9.9 %copy-start.11 = (bf16[8,64,512]{2,1,0:T(8,128)(2,1)}, bf16[8,64,512]{2,1,0:T(8,128)(2,1)S(1)}, u32[]{:S(2)}) copy-start(bf16[8,64,512]{2,1,0:T(8,128)(2,1)S(1)} %fusion.26) | copy-start | bytes 1572868
  264.4 3.5 slice-start
  265.2 2.9 slice-start.1
  265.2 2.9 copy-start.28
  268.1 4.2 copy-start.20
  283.3 1.0 copy-start.18
  283.3 1.8 copy-start.19
  284.3 1.5 copy-start.12
  284.3 1.8 copy-start.14
Sparse Core Ops, SparseCore 0:
  17.6 67.7 all-gather.6
  144.5 64.1 all-gather.8
  211.5 141.2 reduce-scatter.4
  358.9 111.0 reduce-scatter.6
where the time goes:
time: 484 us; the launch traced here: 477 us
  waiting for transfers between devices  218 us (45%)
  matrix products  103 us (21%)
  local copies, waits for them, and re-layouts  55.9 us (12%)
  other arithmetic  51.6 us (11%)
  blocking collectives  32.8 us (7%)
  between operations  14.7 us (3%)
    unnamed x5, waiting for transfers between devices  117 us
    reduce_scatter x1, waiting for transfers between devices, shards(): lax.psum_scatter(row_term(attended, grad_rows, factor), ('dp', 'ctx'), sc...  64 us
    all_gather x2, waiting for transfers between devices, carried_in(): pieces = jax.tree.map(lambda part: lax.all_gather(part, axis), value)  36.6 us
    select_n x28, other arithmetic, turn(): jnp.where(position < mine, new, old)  36.3 us
    all_gather x2, blocking collectives, carried_in(): pieces = jax.tree.map(lambda part: lax.all_gather(part, axis), value)  32.8 us
    dot_general x3, matrix products, block_output(): jnp.einsum('hts,shd->thd', kernel, value_vec, precision=HIGH)  30.1 us
    dynamic_slice x14, local copies, waits for them, and re-layouts, turn(): longer = join(subtotal, jax.tree.map(lambda part: part[position], pieces))  25.4 us
    dot_general x3, matrix products, block_output(): jnp.einsum('the,hed->thd', lifted, prior_state, precision=HIGH)  16.9 us
  transfers between devices with their start and end apart: 4, of which 3 were waited for; matrix products, arithmetic and copies ran while one was open for 29% of the time, Pallas kernels for 0%

commit v1 on v0

v1 whole, which is shorter than its diff:
```python
import functools
import math

import jax
import jax.numpy as jnp
from jax import lax
from jax.experimental import pallas as pl
from jax.experimental.pallas import tpu as pltpu
from jax.sharding import PartitionSpec as P

HEADS = 8
FEAT = 16
HDIM = 64
PAIRS = HEADS // 2
LIFT = 160
SQRT_HALF = 0.7071067811865476
F32 = jnp.float32
BF16 = jnp.bfloat16
MESH = pl.DeviceIdType.MESH
VMEM_LIMIT = 56 * 2**20


def dot_nn(a, b):
    return lax.dot_general(a, b, (((1,), (0,)), ((), ())), preferred_element_type=F32)


def dot_nt(a, b):
    return lax.dot_general(a, b, (((1,), (1,)), ((), ())), preferred_element_type=F32)


def dot_tn(a, b):
    return lax.dot_general(a, b, (((0,), (0,)), ((), ())), preferred_element_type=F32)


def shifted(u, d):
    return u if d == 0 else jnp.concatenate([u[d:], u[:d]], axis=0)


def lift(u):
    count = u.shape[1]
    rows = [u * u * SQRT_HALF]
    for d in range(1, FEAT // 2):
        rows.append(u * shifted(u, d))
    rows.append(u[: FEAT // 2] * u[FEAT // 2 :])
    first = lax.broadcasted_iota(jnp.int32, (8, count), 0) == 0
    rows.append(jnp.where(first, 1.0, 0.0).astype(F32))
    rows.append(u)
    return jnp.concatenate(rows, axis=0)


def unlift(grad, u):
    out = grad[LIFT - FEAT :] + (2.0 * SQRT_HALF) * grad[:FEAT] * u
    for d in range(1, FEAT // 2):
        part = grad[d * FEAT : (d + 1) * FEAT]
        out = out + part * shifted(u, d) + shifted(part * u, FEAT - d)
    half = FEAT // 2
    part = grad[half * FEAT : half * FEAT + half]
    return out + jnp.concatenate([part * u[half:], part * u[:half]], axis=0)


def split(x):
    high = x.astype(BF16)
    return high, (x - high.astype(F32)).astype(BF16)


def stack_rows(rows, count):
    pad = jnp.zeros((16 - len(rows), count), F32)
    return jnp.concatenate([r.astype(F32) for r in rows] + [pad], axis=0).astype(BF16)


def state_kernel(k_ref, v_ref, s_ref, n_ref):
    sums, norms = [], []
    count = k_ref.shape[1]
    for h in range(2):
        lifted = lift(k_ref[h * FEAT : (h + 1) * FEAT, :].astype(F32)).astype(BF16)
        sums.append(dot_nt(lifted, v_ref[h * HDIM : (h + 1) * HDIM, :]))
        norms.append(dot_nt(jnp.ones((8, count), BF16), lifted)[:1])
    s_ref[0] = jnp.concatenate(sums, axis=1)
    n_ref[0] = jnp.concatenate(norms + [jnp.zeros((6, LIFT), F32)], axis=0)


def attend_kernel(q_ref, k_ref, v_ref, g_ref, s_ref, n_ref, a_ref, gq_ref, gk_ref, gv_ref, ds_ref, dn_ref):
    count = q_ref.shape[1]
    later = lax.broadcasted_iota(jnp.int32, (count, count), 1) >= lax.broadcasted_iota(
        jnp.int32, (count, count), 0
    )
    sums, norms = [], []
    for h in range(2):
        small = slice(h * FEAT, (h + 1) * FEAT)
        wide = slice(h * HDIM, (h + 1) * HDIM)
        q, k, v = q_ref[small, :], k_ref[small, :], v_ref[wide, :]
        state = s_ref[0, :, wide].astype(BF16)
        n_high, n_low = split(n_ref[0, h : h + 1, :])
        score = dot_tn(k, q)
        kernel = jnp.where(later, 1.0 + score + 0.5 * score * score, 0.0)
        kernel_b = kernel.astype(BF16)
        u = q.astype(F32)
        lifted = lift(u).astype(BF16)
        top = dot_nn(v, kernel_b) + dot_tn(state, lifted)
        prior = dot_nn(stack_rows([n_high, n_low], LIFT), lifted)
        below = jnp.sum(kernel, axis=0, keepdims=True) + prior[0:1] + prior[1:2]
        inverse = 1.0 / below
        attention = top * inverse
        a_ref[wide, :] = attention.astype(BF16)
        g = g_ref[wide, :] * inverse
        below_grad = -jnp.sum(g * attention, axis=0, keepdims=True)
        g_b = g.astype(BF16)
        b_high, b_low = split(below_grad)
        kernel_grad = dot_tn(v, g_b) + below_grad
        score_grad = jnp.where(later, kernel_grad * (1.0 + score), 0.0).astype(BF16)
        lift_grad = dot_nn(state, g_b) + dot_tn(
            stack_rows([n_high, n_low, n_high], LIFT), stack_rows([b_high, b_high, b_low], count)
        )
        gq_ref[small, :] = ((dot_nn(k, score_grad) + unlift(lift_grad, u)) * 0.5).astype(BF16)
        gk_ref[small, :] = dot_nt(q, score_grad)
        gv_ref[wide, :] = dot_nt(g_b, kernel_b)
        sums.append(dot_nt(lifted, g_b))
        pair = dot_nt(stack_rows([b_high, b_low], count), lifted)
        norms.append(pair[0:1] + pair[1:2])
    ds_ref[0] = jnp.concatenate(sums, axis=1)
    dn_ref[0] = jnp.concatenate(norms + [jnp.zeros((6, LIFT), F32)], axis=0)


def far_kernel(k_ref, v_ref, gk_ref, gv_ref, s_ref, n_ref, pk_ref, pv_ref):
    count = k_ref.shape[1]
    for h in range(2):
        small = slice(h * FEAT, (h + 1) * FEAT)
        wide = slice(h * HDIM, (h + 1) * HDIM)
        u = k_ref[small, :].astype(F32)
        lifted = lift(u).astype(BF16)
        state = s_ref[0, :, wide].astype(BF16)
        n_high, n_low = split(n_ref[0, h : h + 1, :])
        ones = jnp.ones((1, count), F32)
        lift_grad = dot_nn(state, v_ref[wide, :]) + dot_tn(
            stack_rows([n_high, n_low], LIFT), stack_rows([ones, ones], count)
        )
        pk_ref[small, :] = ((gk_ref[small, :] + unlift(lift_grad, u)) * 0.5).astype(BF16)
        pv_ref[wide, :] = (gv_ref[wide, :] + dot_tn(state, lifted)).astype(BF16)


def rows_spec(rows, count):
    return pl.BlockSpec((rows, count), lambda p: (p, 0))


def pair_spec(rows, columns):
    return pl.BlockSpec((1, rows, columns), lambda p: (p, 0, 0))


def flipped(index, bit):
    return index + bit - 2 * bit * lax.rem(lax.div(index, bit), 2)


def bits_of(size):
    return [1 << b for b in range(size.bit_length() - 1)]


def enter(partners):
    barrier = pltpu.get_barrier_semaphore()
    for partner in partners:
        pl.semaphore_signal(barrier, inc=1, device_id=partner, device_id_type=MESH)
    pl.semaphore_wait(barrier, len(partners))


def scan_kernel(size, backward, s_ref, n_ref, so_ref, no_ref, s_sum, n_sum, s_got, n_got, send, recv):
    dp, me = lax.axis_index("dp"), lax.axis_index("ctx")
    bits = bits_of(size)
    partners = [(dp, flipped(me, bit)) for bit in bits]
    enter(partners)
    for at, (bit, partner) in enumerate(zip(bits, partners)):
        last = at == len(bits) - 1
        mine = ((s_ref if at == 0 else s_sum.at[at % 2]), (n_ref if at == 0 else n_sum.at[at % 2]))
        copies = [
            pltpu.make_async_remote_copy(
                src_ref=source,
                dst_ref=target.at[at],
                send_sem=send.at[at, i],
                recv_sem=recv.at[at, i],
                device_id=partner,
                device_id_type=MESH,
            )
            for i, (source, target) in enumerate(zip(mine, (s_got, n_got)))
        ]
        for copy in copies:
            copy.start()
        upper = lax.rem(lax.div(me, bit), 2)
        takes = (1 - upper if backward else upper).astype(F32)
        for copy in copies:
            copy.wait()
        for got, held, total, out in (
            (s_got, mine[0], s_sum, so_ref),
            (n_got, mine[1], n_sum, no_ref),
        ):
            arrived = got[at]
            out[...] = arrived * takes if at == 0 else out[...] + arrived * takes
            if not last:
                total[(at + 1) % 2] = held[...] + arrived


def carried(state, norm, size, backward, call):
    steps = len(bits_of(size))
    vmem = pl.BlockSpec(memory_space=pltpu.VMEM)
    return pl.pallas_call(
        functools.partial(scan_kernel, size, backward),
        out_shape=(
            jax.ShapeDtypeStruct(state.shape, F32),
            jax.ShapeDtypeStruct(norm.shape, F32),
        ),
        in_specs=[vmem, vmem],
        out_specs=(vmem, vmem),
        scratch_shapes=[
            pltpu.VMEM((2,) + state.shape, F32),
            pltpu.VMEM((2,) + norm.shape, F32),
            pltpu.VMEM((steps,) + state.shape, F32),
            pltpu.VMEM((steps,) + norm.shape, F32),
            pltpu.SemaphoreType.DMA((steps, 2)),
            pltpu.SemaphoreType.DMA((steps, 2)),
        ],
        compiler_params=pltpu.CompilerParams(
            collective_id=call, has_side_effects=True, vmem_limit_bytes=VMEM_LIMIT
        ),
    )(state, norm)


def scatter_kernel(dp_size, ctx_size, arrays, *refs):
    dp, me = lax.axis_index("dp"), lax.axis_index("ctx")
    ins, outs = refs[:arrays], refs[arrays : 2 * arrays]
    held = refs[2 * arrays : 4 * arrays]
    got = refs[4 * arrays : 6 * arrays]
    send, recv, load = refs[6 * arrays :]
    dp_bits = [("dp", b) for b in bits_of(dp_size)]
    ctx_bits = [("ctx", b) for b in bits_of(ctx_size)]
    orders = [ctx_bits[:1] + dp_bits + ctx_bits[1:], ctx_bits[:1] + dp_bits[::-1] + ctx_bits[1:]]
    steps = len(orders[0])

    def partner_of(axis, bit):
        return (flipped(dp, bit), me) if axis == "dp" else (dp, flipped(me, bit))

    enter([partner_of(*bit) for bit in orders[0]])
    slots = 1 << steps

    def block_of(order, slot):
        d, c = dp, me
        for at, (axis, bit) in enumerate(order):
            if slot >> (steps - 1 - at) & 1:
                d, c = (flipped(d, bit), c) if axis == "dp" else (d, flipped(c, bit))
        return d * ctx_size + c

    half = slots // 2
    for part, order in enumerate(orders):
        for a in range(arrays):
            buf = 2 * a + part
            rows, columns = held[buf].shape[1:]
            across = pl.ds(part * columns, columns)
            for slot in range(half):
                block = block_of(order, half + slot)
                pltpu.make_async_remote_copy(
                    src_ref=ins[a].at[pl.ds(block * rows, rows), across],
                    dst_ref=got[buf].at[slot],
                    send_sem=send.at[0, buf],
                    recv_sem=recv.at[0, buf],
                    device_id=partner_of(*order[0]),
                    device_id_type=MESH,
                ).start()
            for slot in range(half):
                block = block_of(order, slot)
                pltpu.make_async_copy(
                    ins[a].at[pl.ds(block * rows, rows), across], held[buf].at[slot], load.at[buf]
                ).start()

    def step_copy(at, buf, order):
        keep = slots >> (at + 1)
        if at == 0:
            source, target = held[buf], got[buf].at[pl.ds(0, half)]
        else:
            source = held[buf].at[pl.ds(keep, keep)]
            target = got[buf].at[pl.ds(slots - 2 * keep, keep)]
        return pltpu.make_async_remote_copy(
            src_ref=source,
            dst_ref=target,
            send_sem=send.at[at, buf],
            recv_sem=recv.at[at, buf],
            device_id=partner_of(*order[at]),
            device_id_type=MESH,
        )

    bufs = [(2 * a + part, orders[part]) for a in range(arrays) for part in range(2)]
    for at in range(steps):
        keep = slots >> (at + 1)
        for buf, order in bufs:
            if at == 0:
                pltpu.make_async_copy(held[buf], held[buf], load.at[buf]).wait()
            step_copy(at, buf, order).wait()
            base = slots - 2 * keep
            if at == steps - 1:
                a, part = buf // 2, buf % 2
                columns = held[buf].shape[2]
                outs[a][:, part * columns : (part + 1) * columns] = held[buf][0] + got[buf][base]
                continue
            near = keep // 2

            def add(slot, carry, buf=buf, base=base):
                held[buf][slot] = held[buf][slot] + got[buf][base + slot]
                return carry

            lax.fori_loop(near, keep, add, 0)
            step_copy(at + 1, buf, order).start()
            lax.fori_loop(0, near, add, 0)


def scattered(parts, dp_size, ctx_size, call):
    devices = dp_size * ctx_size
    half = devices // 2
    steps = len(bits_of(devices))
    blocks = [(p.shape[0] // devices, p.shape[1]) for p in parts]
    bufs = [(b[0], b[1] // 2) for b in blocks for _ in range(2)]
    hbm = pl.BlockSpec(memory_space=pl.ANY)
    vmem = pl.BlockSpec(memory_space=pltpu.VMEM)
    return pl.pallas_call(
        functools.partial(scatter_kernel, dp_size, ctx_size, len(parts)),
        out_shape=tuple(jax.ShapeDtypeStruct(b, F32) for b in blocks),
        in_specs=[hbm] * len(parts),
        out_specs=(vmem,) * len(parts),
        scratch_shapes=[pltpu.VMEM((half,) + b, F32) for b in bufs]
        + [pltpu.VMEM((devices - 1,) + b, F32) for b in bufs]
        + [
            pltpu.SemaphoreType.DMA((steps, len(bufs))),
            pltpu.SemaphoreType.DMA((steps, len(bufs))),
            pltpu.SemaphoreType.DMA((len(bufs),)),
        ],
        compiler_params=pltpu.CompilerParams(
            collective_id=call, has_side_effects=True, vmem_limit_bytes=VMEM_LIMIT
        ),
    )(*parts)


def shards(tokens, w_query, w_key, w_value, w_out, grad_out):
    token_rows = tokens.reshape(-1, tokens.shape[-1])
    grad_rows = grad_out.reshape(-1, grad_out.shape[-1])
    count = token_rows.shape[0]
    dp_size, ctx_size = lax.axis_size("dp"), lax.axis_size("ctx")
    narrow, broad = HEADS * FEAT, HEADS * HDIM
    weights = jnp.concatenate([w_query, w_key, w_value], axis=1)
    factor = jnp.where(jnp.arange(weights.shape[1]) < 2 * narrow, 0.5, 1.0)[:, None]
    projected = (
        lax.dot_general(weights, token_rows, (((0,), (1,)), ((), ())), preferred_element_type=F32)
        * factor
    ).astype(BF16)
    q, k, v = projected[:narrow], projected[narrow : 2 * narrow], projected[2 * narrow :]
    g = dot_nt(w_out, grad_rows)
    small, wide = rows_spec(2 * FEAT, count), rows_spec(2 * HDIM, count)
    state_block, norm_block = pair_spec(LIFT, 2 * HDIM), pair_spec(8, LIFT)
    state_shape = jax.ShapeDtypeStruct((PAIRS, LIFT, 2 * HDIM), F32)
    norm_shape = jax.ShapeDtypeStruct((PAIRS, 8, LIFT), F32)
    params = pltpu.CompilerParams(vmem_limit_bytes=VMEM_LIMIT)
    state, norm = pl.pallas_call(
        state_kernel,
        grid=(PAIRS,),
        out_shape=(state_shape, norm_shape),
        in_specs=[small, wide],
        out_specs=(state_block, norm_block),
        compiler_params=params,
    )(k, v)
    state, norm = carried(state, norm, ctx_size, False, 0)
    attended, proj_query, grad_key, grad_value, state, norm = pl.pallas_call(
        attend_kernel,
        grid=(PAIRS,),
        out_shape=(
            jax.ShapeDtypeStruct((broad, count), BF16),
            jax.ShapeDtypeStruct((narrow, count), BF16),
            jax.ShapeDtypeStruct((narrow, count), F32),
            jax.ShapeDtypeStruct((broad, count), F32),
            state_shape,
            norm_shape,
        ),
        in_specs=[small, small, wide, wide, state_block, norm_block],
        out_specs=(wide, small, small, wide, state_block, norm_block),
        compiler_params=params,
    )(q, k, v, g, state, norm)
    state, norm = carried(state, norm, ctx_size, True, 1)
    proj_key, proj_value = pl.pallas_call(
        far_kernel,
        grid=(PAIRS,),
        out_shape=(
            jax.ShapeDtypeStruct((narrow, count), BF16),
            jax.ShapeDtypeStruct((broad, count), BF16),
        ),
        in_specs=[small, wide, small, wide, state_block, norm_block],
        out_specs=(small, wide),
        compiler_params=params,
    )(k, v, grad_key, grad_value, state, norm)
    scale = 1.0 / math.sqrt(dp_size * ctx_size * count)
    stacked = jnp.concatenate([proj_query, proj_key, proj_value], axis=0)
    grad_tokens = lax.dot_general(
        stacked, weights, (((0,), (1,)), ((), ())), preferred_element_type=F32
    ).astype(BF16)
    part_qkv = (
        lax.dot_general(token_rows, stacked, (((0,), (1,)), ((), ())), preferred_element_type=F32)
        * scale
    )
    part_out = dot_nn(attended, grad_rows) * scale
    grad_qkv, grad_w_out = scattered([part_qkv, part_out], dp_size, ctx_size, 2)
    return (grad_tokens.reshape(tokens.shape), grad_qkv, grad_w_out)


def solution(mesh):
    placed = (P("dp", "ctx", None), P(), P(), P(), P(), P("dp", "ctx", None))
    return jax.shard_map(
        shards,
        mesh=mesh,
        in_specs=placed,
        out_specs=(P("dp", "ctx", None), P(("dp", "ctx"), None), P(("dp", "ctx"), None)),
        check_vma=False,
    )
```

time: 484 us -> 188 us (0.39); the launches traced: 477 us -> 188 us
  waiting for transfers between devices: 218 us -> 0 us
  Pallas kernels: 0 us -> 160 us
  matrix products: 103 us -> 15.2 us
  other arithmetic: 51.6 us -> 0.01 us
  local copies, waits for them, and re-layouts: 55.9 us -> 11.9 us
  blocking collectives: 32.8 us -> 0 us
  between operations: 14.7 us -> 0.73 us
    pallas_call x0 -> x6, Pallas kernels: none -> 160 us  [the longest x1 75.5 us: scattered(): pl.pallas_call(functools.partial(scatter_kernel, dp_size, ctx_size, len(p...]
    unnamed x5 -> x0, waiting for transfers between devices: 117 us -> none
    dot_general x23 -> x5, matrix products: 103 us -> 15.2 us  [the longest x1 4.5 us: shards(): lax.dot_general(token_rows, stacked, (((0,), (1,)), ((), ())), preferred_...]
    reduce_scatter x1 -> x0, waiting for transfers between devices: 64 us -> none  [shards(): lax.psum_scatter(row_term(attended, grad_rows, factor), ('dp', 'ctx'), sc...]
    all_gather x2 -> x0, waiting for transfers between devices: 36.6 us -> none  [carried_in(): pieces = jax.tree.map(lambda part: lax.all_gather(part, axis), value)]
    select_n x28 -> x1, other arithmetic: 36.3 us -> 0.01 us  [shards(): jnp.where(jnp.arange(weights.shape[1]) < 2 * narrow, 0.5, 1.0)[:, None]]
    all_gather x2 -> x0, blocking collectives: 32.8 us -> none  [carried_in(): pieces = jax.tree.map(lambda part: lax.all_gather(part, axis), value)]
    dynamic_slice x14 -> x0, local copies, waits for them, and re-layouts: 25.4 us -> none  [turn(): longer = join(subtotal, jax.tree.map(lambda part: part[position], pieces))]
  transfers between devices with their start and end apart: 4 -> 0, of which waited for: 3 -> 0; matrix products, arithmetic and copies ran while one was open for 29% -> 0% of each run, Pallas kernels for 0% -> 0%
where the time goes in v1:
time: 188 us
  Pallas kernels  160 us (85%)
  matrix products  15.2 us (8%)
  local copies, waits for them, and re-layouts  11.9 us (6%)
    pallas_call x1, Pallas kernels, scattered(): pl.pallas_call(functools.partial(scatter_kernel, dp_size, ctx_size, len(p...  75.5 us
    pallas_call x2, Pallas kernels, carried(): pl.pallas_call(functools.partial(scan_kernel, size, backward), out_shape=...  65.6 us
    pallas_call x1, Pallas kernels, shards(): pl.pallas_call(attend_kernel, grid=(PAIRS,), out_shape=(jax.ShapeDtypeStr...  10.7 us
    unnamed x14, local copies, waits for them, and re-layouts  7.49 us
    dot_general x1, matrix products, shards(): lax.dot_general(token_rows, stacked, (((0,), (1,)), ((), ())), preferred_...  4.5 us
    pallas_call x1, Pallas kernels, shards(): pl.pallas_call(far_kernel, grid=(PAIRS,), out_shape=(jax.ShapeDtypeStruct...  4.27 us
    pallas_call x1, Pallas kernels, shards(): pl.pallas_call(state_kernel, grid=(PAIRS,), out_shape=(state_shape, norm_...  3.88 us

profile of v1, /device:TPU:0, one launch (start us, length us, event | category | flops | bytes accessed | tf_op | source)
XLA Modules:
  0.0 187.7 jit_solution(5695103982565924376)
XLA Ops:
  0.6 0.0 copy-start
  0.6 1.3 constant_dynamic-update-slice_fusion.2
  1.9 1.2 constant_dynamic-update-slice_fusion.1
  3.1 1.7 constant_dynamic-update-slice_fusion
  4.8 0.0 copy-done
  4.9 0.0 copy-start.1
  4.9 0.0 copy-start.3
  4.9 1.8 multiply_convert_fusion
  6.7 0.7 fusion.10
  7.4 0.9 slice.14.v_ref
  8.3 0.0 copy-done.1
  8.3 0.0 copy-done.3
  8.3 2.3 %fusion.2.g_ref = f32[512,512]{1,0:T(8,128)} fusion(bf16[512,2048]{1,0:T(8,128)(2,1)S(1)} %copy-done.3, bf16[1,512,2048]{2,1,0:T(8,128)(2,1)S(1)} %copy-done.1), kind=kOutput, calls=%fused_computation.5 | convolution fusion | flops 1073741824 | bytes 5242880 | tf_op jit(solution)/shard_map/dot_general | solution.py:28
  10.7 3.9 %shard_map.85 = (f32[4,160,128]{2,1,0:T(8,128)}, f32[4,8,160]{2,1,0:T(8,128)}) custom-call(bf16[128,512]{1,0:T(8,128)(2,1)} %get-tuple-element.35.k_ref, bf16[512,512]{1,0:T(8,128)(2,1)} %slice.14.v_ref), custom_call_target="tpu_custom_call" | custom-call | tf_op jit(solution)/shard_map/pallas_call | solution.py:355
  14.5 34.4 %shard_map.86 = (f32[4,160,128]{2,1,0:T(8,128)}, f32[4,8,160]{2,1,0:T(8,128)}) custom-call(f32[4,160,128]{2,1,0:T(8,128)} %get-tuple-element.19.s_ref, f32[4,8,160]{2,1,0:T(8,128)} %get-tuple-element.20.n_ref), custom_call_target="tpu_custom_call" | custom-call | tf_op jit(solution)/shard_map/pallas_call | solution.py:202
  48.9 10.7 %shard_map.87 = (bf16[512,512]{1,0:T(8,128)(2,1)}, bf16[128,512]{1,0:T(8,128)(2,1)}, f32[128,512]{1,0:T(8,128)}, f32[512,512]{1,0:T(8,128)}, f32[4,160,128]{2,1,0:T(8,128)}, /*index=5*/f32[4,8,160]{2,1,0:T(8,128)}) custom-call(bf16[128,512]{1,0:T(8,128)(2,1)} %get-tuple-element.36.q_ref, bf16[128,512]{1,0:T(8,128)(2,1)} %get-tuple-element.35.k_ref, ...), custom_call_target="tpu_custom_call" | custom-call | tf_op jit(solution)/shard_map/pallas_call | solution.py:364
  59.6 0.9 constant_dynamic-update-slice_fusion.5
  60.5 31.2 %shard_map.88 = (f32[4,160,128]{2,1,0:T(8,128)}, f32[4,8,160]{2,1,0:T(8,128)}) custom-call(f32[4,160,128]{2,1,0:T(8,128)} %get-tuple-element.26.s_ref, f32[4,8,160]{2,1,0:T(8,128)} %get-tuple-element.27.n_ref), custom_call_target="tpu_custom_call" | custom-call | tf_op jit(solution)/shard_map/pallas_call | solution.py:202
  91.8 4.3 %shard_map.89 = (bf16[128,512]{1,0:T(8,128)(2,1)}, bf16[512,512]{1,0:T(8,128)(2,1)}) custom-call(bf16[128,512]{1,0:T(8,128)(2,1)} %get-tuple-element.35.k_ref, bf16[512,512]{1,0:T(8,128)(2,1)} %slice.14.v_ref, f32[128,512]{1,0:T(8,128)} %get-tuple-element.24.gk_ref, f32[512,512]{1,0:T(8,128)} %get-tuple-element.25.gv_ref, ...), custom_call_target="tpu_custom_call" | custom-call | tf_op jit(solution)/shard_map/pallas_call | solution.py:380
  96.1 0.9 constant_dynamic-update-slice_fusion.4
  97.0 1.1 constant_dynamic-update-slice_fusion.3
  98.1 3.2 %fusion = bf16[1,512,2048]{2,1,0:T(8,128)(2,1)} fusion(bf16[768,512]{1,0:T(8,128)(2,1)S(1)} %constant_dynamic-update-slice_fusion.3, bf16[2048,768]{1,0:T(8,128)(2,1)S(1)} %constant_dynamic-update-slice_fusion), kind=kOutput, calls=%fused_computation.3 | convolution fusion | flops 1611661312 | bytes 6029312 | tf_op jit(solution)/shard_map/dot_general | solution.py:393
  101.2 0.0 copy-start.2
  101.2 4.5 %multiply_bitcast_fusion.refs_0_ = f32[2048,768]{1,0:T(8,128)} fusion(bf16[768,512]{1,0:T(8,128)(2,1)S(1)} %constant_dynamic-update-slice_fusion.3, bf16[1,512,2048]{2,1,0:T(8,128)(2,1)S(1)} %copy-done), kind=kOutput, calls=%fused_computation | convolution fusion | flops 1612185600 | bytes 9175040 | tf_op jit(solution)/shard_map/dot_general | solution.py:397
  105.7 0.0 copy-done.2
  105.7 3.3 %convolution_multiply_fusion.refs_1_ = f32[512,2048]{1,0:T(8,128)} fusion(bf16[512,512]{1,0:T(8,128)(2,1)S(1)} %copy-done.2, bf16[1,512,2048]{2,1,0:T(8,128)(2,1)S(1)} %copy-done.1), kind=kOutput, calls=%fused_computation.1 | convolution fusion | flops 1074790400 | bytes 6815744 | tf_op jit(solution)/shard_map/dot_general | solution.py:24
  109.0 75.5 %shard_map.90 = (f32[64,768]{1,0:T(8,128)}, f32[16,2048]{1,0:T(8,128)}) custom-call(f32[2048,768]{1,0:T(8,128)} %multiply_bitcast_fusion.refs_0_, f32[512,2048]{1,0:T(8,128)} %convolution_multiply_fusion.refs_1_), custom_call_target="tpu_custom_call" | custom-call | tf_op jit(solution)/shard_map/pallas_call | solution.py:318
  184.5 1.6 copy.17
  186.1 1.6 copy.18
  (1 shorter events, 0.0 us)
Async XLA Ops:
  0.6 4.2 %copy-start = (bf16[1,512,2048]{2,1,0:T(8,128)(2,1)S(1)}, bf16[1,512,2048]{2,1,0:T(8,128)(2,1)}, u32[]{:S(2)}) copy-start(bf16[1,512,2048]{2,1,0:T(8,128)(2,1)} %param.6) | copy-start | bytes 6291460
  4.9 3.5 %copy-start.1 = (bf16[1,512,2048]{2,1,0:T(8,128)(2,1)S(1)}, bf16[1,512,2048]{2,1,0:T(8,128)(2,1)}, u32[]{:S(2)}) copy-start(bf16[1,512,2048]{2,1,0:T(8,128)(2,1)} %param.11) | copy-start | bytes 6291460
  4.9 3.5 %copy-start.3 = (bf16[512,2048]{1,0:T(8,128)(2,1)S(1)}, bf16[512,2048]{1,0:T(8,128)(2,1)}, u32[]{:S(2)}) copy-start(bf16[512,2048]{1,0:T(8,128)(2,1)} %param.10) | copy-start | bytes 6291460
  101.2 4.5 %copy-start.2 = (bf16[512,512]{1,0:T(8,128)(2,1)S(1)}, bf16[512,512]{1,0:T(8,128)(2,1)}, u32[]{:S(2)}) copy-start(bf16[512,512]{1,0:T(8,128)(2,1)} %get-tuple-element.32) | copy-start | bytes 1572868
